TPU v7x, 128 devices: a whole 4x4x4 slice. The times are simulated.
128 devices in a mesh: fsdp: 16 (over z, y), tensor: 8 (over x, core).
Axes of the slice: x: 4, y: 4, z: 4, core: 2. Of those that a mesh axis runs over, the one named last changes fastest.
Arguments:
- momentum: float32 [8192, 26624], P('fsdp', 'tensor'), may hold values from -180 to 180
- gradient: bfloat16 [8192, 26624], P('fsdp', 'tensor'), may hold values from -180 to 180
- factor: float32 [26624, 128], P('tensor'), may hold values from -1 to 1
Outputs:
- new_momentum: float32 [8192, 26624], P('fsdp', 'tensor')
- left_basis: float32 [8192, 128], P('fsdp')
- new_factor: float32 [26624, 128], P('tensor')
All inputs are finite; a program needn't handle non-finite values.
Results may differ from a plain program's by a relative error of at most 0.0003.
Values sent between devices are 32-bit elements; how exact they have to be, the bound alone decides.
A program may use at most 64 MiB of HBM per device.

v0:
```python
import jax
import jax.numpy as jnp
from jax import lax
from jax.experimental import pallas as pl
from jax.experimental.pallas import tpu as pltpu
from jax.sharding import PartitionSpec as P

MESH = pl.DeviceIdType.MESH
HIGHEST = lax.Precision.HIGHEST
f32, bf16 = jnp.float32, jnp.bfloat16
momentum_decay = 0.9

ROWS, COLS, RANK = 512, 3328, 128
FSDP, TENSOR, SIDE = 16, 8, 4
CHUNKS = 4
CHUNK = ROWS // CHUNKS
GROUPS = ((0, 896, "y", "z"), (896, 896, "z", "y"), (1792, 768, "y", "z"), (2560, 768, "z", "y"))
WIDE = 256
PANEL, STRIP = 64, 16
PIECES = (8, 1, 2)
PLAN = (
    "gram1 m0 f0 m1", "f1 m2 m3 share1", "f2 f3 take1", "chol1:0=s0,0=s1,7=s2,7=s3", "gram2 t0 t1 t2", "t3 q0 q1 share2",
    "q2 q3 take2 chol2",
)


def dot(left, right, precision=None):
    return jnp.dot(left, right, precision=precision, preferred_element_type=f32)


def dot_rows(left, right, precision=None):
    return lax.dot_general(left, right, (((0,), (0,)), ((), ())), precision=precision, preferred_element_type=f32)


def dot_lanes(left, right, precision=None):
    return lax.dot_general(left, right, (((1,), (1,)), ((), ())), precision=precision, preferred_element_type=f32)


def split3(x):
    first = x.astype(bf16)
    rest = x - first.astype(f32)
    second = rest.astype(bf16)
    third = (rest - second.astype(f32)).astype(bf16)
    return first, second, third


def split2(x):
    first = x.astype(bf16)
    return first, (x - first.astype(f32)).astype(bf16)


def tiles(width, step=WIDE):
    return [(at, min(step, width - at)) for at in range(0, width, step)]


def cholesky_inverse(work, gram, between):
    row = lax.broadcasted_iota(jnp.int32, (8, RANK), 0)
    spread = lambda x: jnp.broadcast_to(x, (8, RANK))
    row_all = lax.broadcasted_iota(jnp.int32, (RANK, RANK), 0)
    lane_all = lax.broadcasted_iota(jnp.int32, (RANK, RANK), 1)
    work[:, :RANK] = gram
    work[:, RANK:] = jnp.where(row_all == lane_all, 1.0, 0.0)
    count = PANEL // 8
    for start in range(0, RANK, PANEL):
        left = [work[start + 8 * v : start + 8 * v + 8, :RANK] for v in range(count)]
        right = [work[start + 8 * v : start + 8 * v + 8, RANK:] for v in range(count)]
        scale = [jnp.ones((8, RANK), f32) for _ in range(count)]
        for strip in range(0, PANEL, STRIP):
            column = {}
            for m in range(strip, strip + STRIP):
                for v in range(strip // 8, count):
                    column[m, v] = spread(left[v][:, start + m : start + m + 1])
            for i in range(strip, strip + STRIP):
                at, r = i // 8, i % 8
                pivot = spread(column[i, at][r : r + 1, :])
                inverse = 1.0 / pivot
                scale[at] = jnp.where(row == r, pivot, scale[at])
                later = range(i + 1, strip + STRIP)
                tops = {m: spread(column[m, at][r : r + 1, :]) for m in later}
                left_top, right_top = spread(left[at][r : r + 1, :]), spread(right[at][r : r + 1, :])
                for v in range(at, count):
                    if v == at and r == 7:
                        continue
                    ratio = column[i, v] * inverse
                    if v == at:
                        ratio = jnp.where(row > r, ratio, 0.0)
                    for m in later:
                        column[m, v] = column[m, v] - ratio * tops[m]
                    left[v] = left[v] - ratio * left_top
                    right[v] = right[v] - ratio * right_top
            between((start + strip) // STRIP)
        scale = [lax.rsqrt(v) for v in scale]
        upper = jnp.concatenate([v * w for v, w in zip(left, scale)], axis=0)
        both = jnp.concatenate([upper, jnp.concatenate([v * w for v, w in zip(right, scale)], axis=0)], axis=1)
        work[start : start + PANEL, :] = both
        below = start + PANEL
        if below < RANK:
            lane = lax.broadcasted_iota(jnp.int32, (PANEL, RANK), 1)
            update = dot_rows(jnp.where(lane >= below, upper, 0.0), both, HIGHEST)
            work[below:, :] = work[below:, :] - update[below:, :]
    return work[:, RANK:]


def kernel(
    momentum, gradient, factor, summed, left_basis, new_factor,
    grad, fac, s1, s2, s3, f12, f3, part, core_in, cross, a_full, grams, gram_all, gram_part, work, bt, rt, rsa, rsb,
    squares, right_rows,
    load_sem, a_send, a_recv, g_send, g_recv, r_send, r_recv,
):
    f, t = lax.axis_index("fsdp"), lax.axis_index("tensor")
    z, y = f // SIDE, lax.rem(f, SIDE)
    x, c = t // 2, lax.rem(t, 2)
    other_core = (f, x * 2 + 1 - c)
    x_peers = [(f, lax.rem(x + k, SIDE) * 2 + c) for k in range(1, SIDE)]
    far = lambda k: min(k, SIDE - k)
    hops = sorted(((j, k) for j in range(SIDE) for k in range(SIDE) if j + k), key=lambda v: (-far(v[0]) - far(v[1]), v))
    f_peers = [(lax.rem(z + j, SIDE) * SIDE + lax.rem(y + k, SIDE), t) for j, k in hops]
    hops = sorted(((j, k) for j in range(SIDE) for k in range(2) if j + k), key=lambda v: (-far(v[0]), v))
    t_peers = [(f, lax.rem(x + j, SIDE) * 2 + lax.rem(c + k, 2)) for j, k in hops]
    along = {
        "y": (y, [lax.rem(y + k, SIDE) for k in range(1, SIDE)], lambda v: (z * SIDE + v, t)),
        "z": (z, [lax.rem(z + k, SIDE) for k in range(1, SIDE)], lambda v: (v * SIDE + y, t)),
    }
    sent = []

    def remote(src, dst, send, recv, to):
        copy = pltpu.make_async_remote_copy(
            src_ref=src, dst_ref=dst, send_sem=send, recv_sem=recv, device_id=to, device_id_type=MESH
        )
        copy.start()
        sent.append(copy)
        return copy

    loads = [pltpu.make_async_copy(factor, fac, load_sem.at[2 * CHUNKS])]
    for i in range(CHUNKS):
        rows = pl.ds(i * CHUNK, CHUNK)
        loads.append(pltpu.make_async_copy(momentum.at[rows], summed.at[rows], load_sem.at[2 * i]))
        loads.append(pltpu.make_async_copy(gradient.at[rows], grad.at[rows], load_sem.at[2 * i + 1]))
    for load in loads:
        load.start()

    barrier = pltpu.get_barrier_semaphore()
    greeted = t_peers + f_peers
    for peer in greeted:
        pl.semaphore_signal(barrier, inc=1, device_id=peer, device_id_type=MESH)

    def add_and_split(i, at, width):
        where = (pl.ds(i * CHUNK, CHUNK), pl.ds(at, width))
        total = summed[where] + grad[where].astype(f32)
        summed[where] = total
        s1[where], s2[where], s3[where] = split3(total)

    def wait_rows(i):
        loads[1 + 2 * i].wait()
        loads[2 + 2 * i].wait()

    loads[0].wait()
    for at, width in tiles(COLS):
        here = pl.ds(at, width)
        f12[here, :RANK], f12[here, RANK:], f3[here, :] = split3(fac[here, :])
    wait_rows(0)
    for at, width in tiles(COLS):
        add_and_split(0, at, width)

    half = CHUNK // 2
    core_copies, cross_copies, back_copies = [], [], []

    def pass_across(i):
        core_copies[i].wait_recv()
        cross[i, x] = part[i, pl.ds(c * half, half)] + core_in[i]
        cross_copies.append(
            [
                remote(cross.at[i, x], cross.at[i, x], a_send.at[CHUNKS + 3 * i + k], a_recv.at[CHUNKS + 3 * i + k], peer)
                for k, peer in enumerate(x_peers)
            ]
        )

    def pass_back(i):
        for copy in cross_copies[i]:
            copy.wait_recv()
        mine = pl.ds(i * CHUNK + c * half, half)
        a_full[mine, :] = (cross[i, 0] + cross[i, 1]) + (cross[i, 2] + cross[i, 3])
        back_copies.append(
            remote(a_full.at[mine], a_full.at[mine], a_send.at[4 * CHUNKS + i], a_recv.at[4 * CHUNKS + i], other_core)
        )

    for i in range(CHUNKS):
        rows = pl.ds(i * CHUNK, CHUNK)
        if i + 1 < CHUNKS:
            wait_rows(i + 1)
        pair = jnp.zeros((CHUNK, 2 * RANK), f32)
        small = jnp.zeros((CHUNK, RANK), f32)
        for at, width in tiles(COLS):
            if i + 1 < CHUNKS:
                add_and_split(i + 1, at, width)
            here = pl.ds(at, width)
            pair = pair + (dot(s1[rows, here], f12[here, :]) + dot(s2[rows, here], f12[here, :]))
            small = small + (dot(s1[rows, here], f3[here, :]) + dot(s3[rows, here], f12[here, :RANK]))
        part[i] = pair[:, :RANK] + (pair[:, RANK:] + small)
        if i == 0:
            pl.semaphore_wait(barrier, len(greeted))
        core_copies.append(
            remote(part.at[i, pl.ds((1 - c) * half, half)], core_in.at[i], a_send.at[i], a_recv.at[i], other_core)
        )
        if i > 0:
            pass_across(i - 1)
    pass_across(CHUNKS - 1)
    for i in range(CHUNKS):
        pass_back(i)
    for copy in back_copies:
        copy.wait_recv()

    def gram_send(k, rows):
        gram_part[...] = dot_rows(rows, rows, HIGHEST)
        share = RANK // TENSOR
        grams[k, f] = gram_part[pl.ds(pl.multiple_of(t * share, share), share), :]
        return [
            remote(grams.at[k, f], grams.at[k, f], g_send.at[k, n], g_recv.at[k, n], peer) for n, peer in enumerate(f_peers)
        ]

    def gram_share(k, copies):
        for copy in copies:
            copy.wait_recv()
        total = grams[k, 0]
        for n in range(1, FSDP):
            total = total + grams[k, n]
        gram_all[k, t] = total
        return [
            remote(gram_all.at[k, t], gram_all.at[k, t], g_send.at[k, FSDP - 1 + n], g_recv.at[k, FSDP - 1 + n], peer)
            for n, peer in enumerate(t_peers)
        ]

    def gram_take(k, copies):
        for copy in copies:
            copy.wait_recv()
        return gram_all[k].reshape(RANK, RANK)

    a = a_full[...]
    at1, at2, at3 = split3(a.T)
    stack = jnp.concatenate([at1, at2, at3], axis=0)
    chunk_rows = RANK // SIDE
    piece_rows = chunk_rows // SIDE
    moves = {}

    def cols_of(g):
        return pl.ds(GROUPS[g][0], GROUPS[g][1])

    def place(g):
        own = pl.multiple_of(along[GROUPS[g][2]][0] * chunk_rows, chunk_rows)
        return own, pl.multiple_of(own + along[GROUPS[g][3]][0] * piece_rows, piece_rows)

    def multiply(g):
        start, size, _, _ = GROUPS[g]
        for at, width in tiles(size):
            cols = pl.ds(start + at, width)
            one = dot(stack, s1[:, cols])
            two = dot(stack[: 2 * RANK], s2[:, cols])
            three = dot(at1, s3[:, cols])
            low = one[2 * RANK :] + (two[RANK:] + three)
            bt[:, cols] = one[:RANK] + ((one[RANK : 2 * RANK] + two[:RANK]) + low)

    def first_send(g):
        _, peers, where = along[GROUPS[g][2]]
        cols = cols_of(g)
        moves[0, g] = [
            remote(
                bt.at[pl.ds(v * chunk_rows, chunk_rows), cols], rsa.at[k, :, cols], r_send.at[0, g, k], r_recv.at[0, g, k], where(v)
            )
            for k, v in enumerate(peers)
        ]

    def second_send(g):
        for copy in moves[0, g]:
            copy.wait_recv()
        own, _ = place(g)
        cols = cols_of(g)
        mine = pl.ds(own, chunk_rows)
        bt[mine, cols] = (bt[mine, cols] + rsa[0, :, cols]) + (rsa[1, :, cols] + rsa[2, :, cols])
        _, peers, where = along[GROUPS[g][3]]
        moves[1, g] = [
            remote(
                bt.at[pl.ds(own + v * piece_rows, piece_rows), cols],
                rsb.at[k, :, cols], r_send.at[1, g, k], r_recv.at[1, g, k], where(v),
            )
            for k, v in enumerate(peers)
        ]

    def third_send(g):
        for copy in moves[1, g]:
            copy.wait_recv()
        _, at = place(g)
        cols = cols_of(g)
        mine = pl.ds(at, piece_rows)
        rt[mine, cols] = (bt[mine, cols] + rsb[0, :, cols]) + (rsb[1, :, cols] + rsb[2, :, cols])
        _, peers, where = along[GROUPS[g][3]]
        moves[2, g] = [
            remote(rt.at[mine, cols], rt.at[mine, cols], r_send.at[2, g, k], r_recv.at[2, g, k], where(v))
            for k, v in enumerate(peers)
        ]

    def fourth_send(g):
        for copy in moves[2, g]:
            copy.wait_recv()
        own, _ = place(g)
        cols = cols_of(g)
        mine = pl.ds(own, chunk_rows)
        _, peers, where = along[GROUPS[g][2]]
        moves[3, g] = [
            remote(rt.at[mine, cols], rt.at[mine, cols], r_send.at[3, g, k], r_recv.at[3, g, k], where(v))
            for k, v in enumerate(peers)
        ]

    steps = {"m": multiply, "f": first_send, "s": second_send, "t": third_send, "q": fourth_send}
    state = {"rows0": a}

    def round_step(name, k, inside):
        if name == "gram":
            if k == 1:
                state["rows1"] = dot_lanes(a, state["inverse0"], HIGHEST)
            state["sent"] = gram_send(k, state["rows%d" % k])
        elif name == "share":
            state["sent"] = gram_share(k, state["sent"])
        elif name == "take":
            state["gram"] = gram_take(k, state["sent"])
        else:
            state["inverse%d" % k] = cholesky_inverse(work, state["gram"], inside)

    for word in " ".join(PLAN).split():
        word, _, hooks = word.partition(":")

        def inside(strip, hooks=hooks):
            for hook in hooks.split(","):
                when, _, step = hook.partition("=")
                if when == str(strip):
                    steps[step[0]](int(step[1]))

        if word[0] in steps and len(word) == 2:
            steps[word[0]](int(word[1]))
        else:
            round_step(word[:-1], int(word[-1]) - 1, inside)
    second_left, inverse_one, inverse_two = state["rows1"], state["inverse0"], state["inverse1"]
    turn = dot(inverse_two, inverse_one, HIGHEST)
    basis = dot_lanes(second_left, inverse_two, HIGHEST)
    left_basis[...] = basis
    q12 = jnp.concatenate(split2(basis * (1.0 - momentum_decay)), axis=1)
    t1, t2, t3 = split3(turn)
    t12 = jnp.concatenate([t1, t2], axis=1)
    t13 = jnp.concatenate([t1, t3], axis=1)
    energy = jnp.zeros((RANK, RANK), f32)
    for g, (start, size, _, _) in enumerate(GROUPS):
        for copy in moves[3, g]:
            copy.wait_recv()
        for at, width in tiles(size):
            cols = pl.ds(start + at, width)
            r1, r2, r3 = split3(rt[:, cols])
            right = dot(t12, jnp.concatenate([r1, r1], axis=0)) + (
                dot(t12, jnp.concatenate([r2, r2], axis=0)) + dot(t13, jnp.concatenate([r3, r1], axis=0))
            )
            right_rows[:, cols] = right
            for lane in range(0, width, RANK):
                tile = right[:, lane : lane + RANK]
                energy = energy + tile * tile
    squares[t] = dot_lanes(jnp.ones((8, RANK), f32), energy, HIGHEST)
    last = [
        remote(squares.at[t], squares.at[t], a_send.at[5 * CHUNKS + n], a_recv.at[5 * CHUNKS + n], peer)
        for n, peer in enumerate(t_peers)
    ]
    for n, (start, size, _, _) in enumerate(GROUPS):
        for at, width in tiles(size):
            cols = pl.ds(start + at, width)
            right = right_rows[:, cols]
            rounded = right.astype(bf16)
            summed[:, cols] = summed[:, cols] - dot(q12, jnp.concatenate([rounded, rounded], axis=0))
            new_factor[cols, :] = right.T
    for copy in last:
        copy.wait_recv()
    total = squares[0]
    for n in range(1, TENSOR):
        total = total + squares[n]
    new_factor[...] = new_factor[...] * lax.rsqrt(total[:1] + 1e-06)
    for copy in sent:
        copy.wait_send()


def write_out(*refs):
    copies = []
    for source, target, pieces in zip(refs[:3], refs[3:6], PIECES):
        size = source.shape[0] // pieces
        for k in range(pieces):
            rows = pl.ds(k * size, size)
            copies.append(pltpu.make_async_copy(source.at[rows], target.at[rows], refs[6].at[len(copies)]))
            copies[-1].start()
    for copy in copies:
        copy.wait()


def per_device(momentum, gradient, factor):
    dma = pltpu.SemaphoreType.DMA
    results = pl.pallas_call(
        kernel,
        out_shape=(
            pltpu.VMEM((ROWS, COLS), f32),
            pltpu.VMEM((ROWS, RANK), f32),
            pltpu.VMEM((COLS, RANK), f32),
        ),
        in_specs=[pl.BlockSpec(memory_space=pltpu.HBM)] * 3,
        out_specs=[pl.BlockSpec(memory_space=pltpu.VMEM)] * 3,
        scratch_shapes=[
            pltpu.VMEM((ROWS, COLS), bf16),
            pltpu.VMEM((COLS, RANK), f32),
            pltpu.VMEM((ROWS, COLS), bf16),
            pltpu.VMEM((ROWS, COLS), bf16),
            pltpu.VMEM((ROWS, COLS), bf16),
            pltpu.VMEM((COLS, 2 * RANK), bf16),
            pltpu.VMEM((COLS, RANK), bf16),
            pltpu.VMEM((CHUNKS, CHUNK, RANK), f32),
            pltpu.VMEM((CHUNKS, CHUNK // 2, RANK), f32),
            pltpu.VMEM((CHUNKS, SIDE, CHUNK // 2, RANK), f32),
            pltpu.VMEM((ROWS, RANK), f32),
            pltpu.VMEM((2, FSDP, RANK // TENSOR, RANK), f32),
            pltpu.VMEM((2, TENSOR, RANK // TENSOR, RANK), f32),
            pltpu.VMEM((RANK, RANK), f32),
            pltpu.VMEM((RANK, 2 * RANK), f32),
            pltpu.VMEM((RANK, COLS), f32),
            pltpu.VMEM((RANK, COLS), f32),
            pltpu.VMEM((SIDE - 1, RANK // SIDE, COLS), f32),
            pltpu.VMEM((SIDE - 1, RANK // FSDP, COLS), f32),
            pltpu.VMEM((TENSOR, 8, RANK), f32),
            pltpu.VMEM((RANK, COLS), f32),
            dma((2 * CHUNKS + 1,)),
            dma((5 * CHUNKS + TENSOR - 1,)),
            dma((5 * CHUNKS + TENSOR - 1,)),
            dma((2, FSDP + TENSOR - 2)),
            dma((2, FSDP + TENSOR - 2)),
            dma((4, len(GROUPS), SIDE - 1)),
            dma((4, len(GROUPS), SIDE - 1)),
        ],
        compiler_params=pltpu.CompilerParams(collective_id=0, has_side_effects=True, vmem_limit_bytes=44 << 20),
        cost_estimate=pl.CostEstimate(flops=8 * 10**9, bytes_accessed=20 * 10**6, transcendentals=0),
        name="dion_update",
    )(*(pltpu.with_memory_space_constraint(v, pltpu.HBM) for v in (momentum, gradient, factor)))
    return pl.pallas_call(
        write_out,
        out_shape=tuple(jax.ShapeDtypeStruct(v.shape, v.dtype) for v in results),
        in_specs=[pl.BlockSpec(memory_space=pl.ANY)] * 3,
        out_specs=[pl.BlockSpec(memory_space=pl.ANY)] * 3,
        scratch_shapes=[dma((sum(PIECES),))],
        compiler_params=pltpu.CompilerParams(vmem_limit_bytes=1 << 20),
        cost_estimate=pl.CostEstimate(flops=0, bytes_accessed=9 * 10**6, transcendentals=0),
        name="write_out",
    )(*(pltpu.with_memory_space_constraint(v, pltpu.VMEM) for v in results))


def solution(mesh):
    return jax.shard_map(
        per_device,
        mesh=mesh,
        in_specs=(P("fsdp", "tensor"), P("fsdp", "tensor"), P("tensor", None)),
        out_specs=(P("fsdp", "tensor"), P("fsdp", None), P("tensor", None)),
        check_vma=False,
    )
```

profile of v0, /device:TPU:1, one launch (start us, length us, event | category | flops | bytes accessed | tf_op | source)
XLA Modules:
  0.0 64.9 jit_solution(6522282532510056131)
XLA Ops:
  0.6 60.6 %dion_update.1 = (f32[512,3328]{1,0:T(8,128)S(1)}, f32[512,128]{1,0:T(8,128)S(1)}, f32[3328,128]{1,0:T(8,128)S(1)}) custom-call(f32[512,3328]{1,0:T(8,128)} %momentum.1, bf16[512,3328]{1,0:T(8,128)(2,1)} %gradient.1, f32[3328,128]{1,0:T(8,128)} %factor.1), custom_call_target="tpu_custom_call" | custom-call | flops 8000000000 | bytes 20000000 | tf_op jit(solution)/shard_map/dion_update/pallas_call | solution.py:399
  61.3 3.5 %write_out.1 = (f32[512,3328]{1,0:T(8,128)}, f32[512,128]{1,0:T(8,128)}, f32[3328,128]{1,0:T(8,128)}) custom-call(f32[512,3328]{1,0:T(8,128)S(1)} %get-tuple-element.6.refs_0_, f32[512,128]{1,0:T(8,128)S(1)} %get-tuple-element.7.refs_1_, f32[3328,128]{1,0:T(8,128)S(1)} %get-tuple-element.8.refs_2_), custom_call_target="tpu_custom_call" | custom-call | bytes 9000000 | tf_op jit(solution)/shard_map/write_out/pallas_call | solution.py:442
where the time goes:
time: 65 us; the launch traced here: 64.9 us
  Pallas kernels  64.1 us (99%)
  between operations  0.8 us (1%)
    pallas_call x1, Pallas kernels, per_device(): pl.pallas_call(kernel, out_shape=(pltpu.VMEM((ROWS, COLS), f32), pltpu.VM...  60.6 us
    pallas_call x1, Pallas kernels, per_device(): pl.pallas_call(write_out, out_shape=tuple((jax.ShapeDtypeStruct(v.shape,...  3.5 us

commit v1 on v0

--- a/solution.py
+++ b/solution.py
@@ -343,6 +343,10 @@
     basis = dot_lanes(second_left, inverse_two, HIGHEST)
     left_basis[...] = basis
     q12 = jnp.concatenate(split2(basis * (1.0 - momentum_decay)), axis=1)
+    gathers = [copy for g in range(len(GROUPS)) for copy in moves[3, g]]
+    for copy in sent:
+        if not any(copy is gather for gather in gathers):
+            copy.wait_send()
     t1, t2, t3 = split3(turn)
     t12 = jnp.concatenate([t1, t2], axis=1)
     t13 = jnp.concatenate([t1, t3], axis=1)
@@ -372,13 +376,15 @@
             rounded = right.astype(bf16)
             summed[:, cols] = summed[:, cols] - dot(q12, jnp.concatenate([rounded, rounded], axis=0))
             new_factor[cols, :] = right.T
+    for copy in gathers:
+        copy.wait_send()
     for copy in last:
         copy.wait_recv()
     total = squares[0]
     for n in range(1, TENSOR):
         total = total + squares[n]
     new_factor[...] = new_factor[...] * lax.rsqrt(total[:1] + 1e-06)
-    for copy in sent:
+    for copy in last:
         copy.wait_send()
 
 

time: 65 us -> 64.9 us (level)
  no operation moved by 1% of the time
where the time goes in v1:
time: 64.9 us; the launch traced here: 64.8 us
  Pallas kernels  64 us (99%)
  between operations  0.8 us (1%)
    pallas_call x1, Pallas kernels, per_device(): pl.pallas_call(kernel, out_shape=(pltpu.VMEM((ROWS, COLS), f32), pltpu.VM...  60.5 us
    pallas_call x1, Pallas kernels, per_device(): pl.pallas_call(write_out, out_shape=tuple((jax.ShapeDtypeStruct(v.shape,...  3.5 us

profile of v1, /device:TPU:1, one launch (start us, length us, event | category | flops | bytes accessed | tf_op | source)
XLA Modules:
  0.0 64.8 jit_solution(5868715726170674316)
XLA Ops:
  0.6 60.5 %dion_update.1 = (f32[512,3328]{1,0:T(8,128)S(1)}, f32[512,128]{1,0:T(8,128)S(1)}, f32[3328,128]{1,0:T(8,128)S(1)}) custom-call(f32[512,3328]{1,0:T(8,128)} %momentum.1, bf16[512,3328]{1,0:T(8,128)(2,1)} %gradient.1, f32[3328,128]{1,0:T(8,128)} %factor.1), custom_call_target="tpu_custom_call" | custom-call | flops 8000000000 | bytes 20000000 | tf_op jit(solution)/shard_map/dion_update/pallas_call | solution.py:405
  61.1 3.5 %write_out.1 = (f32[512,3328]{1,0:T(8,128)}, f32[512,128]{1,0:T(8,128)}, f32[3328,128]{1,0:T(8,128)}) custom-call(f32[512,3328]{1,0:T(8,128)S(1)} %get-tuple-element.6.refs_0_, f32[512,128]{1,0:T(8,128)S(1)} %get-tuple-element.7.refs_1_, f32[3328,128]{1,0:T(8,128)S(1)} %get-tuple-element.8.refs_2_), custom_call_target="tpu_custom_call" | custom-call | bytes 9000000 | tf_op jit(solution)/shard_map/write_out/pallas_call | solution.py:448
